TPU v7x, 128 devices: a whole 4x4x4 slice. The times are simulated.
128 devices in a mesh: row: 16 (over z, y), col: 8 (over x, core).
Axes of the slice: x: 4, y: 4, z: 4, core: 2. Of those that a mesh axis runs over, the one named last changes fastest.
Arguments:
- rhs: float32 [1, 128, 256, 4096], P(None, ('row', 'col')), may hold values from -6 to 6
- panel: bfloat16 [1, 128, 256, 1024], P(None, ('row', 'col')), may hold values from -0.375 to 0.375
- diag_inverse: float32 [4, 256, 256], replicated, may hold values from -1 to 1.5, as said below
Outputs:
- solution: float32 [1024, 4096], replicated
- trailing: float32 [1, 128, 256, 4096], P(None, ('row', 'col'))
Inputs may be any that keep to these rules, and one draw needn't show every extreme that they name: `diag_inverse`: each of the 4 blocks is lower triangular with diagonal entries between 0.5 and 1.5.
All inputs are finite; a program needn't handle non-finite values.
Results may differ from a plain program's by a relative error of at most 0.0043.
Values may be sent and summed in bfloat16 or wider, within the bound.
A program may use at most 192 MiB of HBM per device.

v0:
```python
import jax
import jax.numpy as jnp
from jax import lax
from jax.sharding import PartitionSpec as P


def spread(block, axis, holder):
    block = jnp.where(lax.axis_index(axis) == holder, block, jnp.zeros_like(block))
    return lax.psum(block, axis)


def apply_step(work, panel, solved_low, numbers, step, width):
    local_blocks = work.shape[0]
    shots = work.shape[3]
    columns = panel[:, 0, :, step * width : (step + 1) * width].reshape(local_blocks * width, width)
    update = jnp.dot(columns, solved_low, preferred_element_type=jnp.float32).reshape(
        local_blocks, 1, width, shots
    )
    below = (numbers > step)[:, None, None, None]
    return work - jnp.where(below, update, jnp.zeros_like(update))


def body(rhs, panel, diag_inverse):
    local_blocks = rhs.shape[0]
    width = rhs.shape[2]
    steps_total = diag_inverse.shape[0]
    col_count = lax.axis_size("col")
    dev_count = lax.axis_size("row") * col_count
    place = lax.axis_index("row") * col_count + lax.axis_index("col")
    numbers = jnp.arange(local_blocks, dtype=jnp.int32) * dev_count + place
    work = rhs
    solved_list = []
    for step in range(steps_total):
        candidate = jnp.dot(
            diag_inverse[step],
            work[0, 0],
            precision=lax.Precision.HIGHEST,
            preferred_element_type=jnp.float32,
        )
        solved = spread(candidate, ("row", "col"), step)
        solved_list.append(solved)
        work = apply_step(work, panel, solved.astype(jnp.bfloat16), numbers, step, width)
    solution = jnp.concatenate(solved_list, axis=0)
    return (solution, work)


def solution(mesh):
    in_specs = (P(None, ("row", "col"), None, None), P(None, ("row", "col"), None, None), P())
    out_specs = (P(), P(None, ("row", "col"), None, None))
    return jax.shard_map(body, mesh=mesh, in_specs=in_specs, out_specs=out_specs, check_vma=False)
```

profile of v0, /device:TPU:23, one launch (start us, length us, event | category | flops | bytes accessed | tf_op | source)
XLA Modules:
  0.0 684.2 jit_solution(5917219070847153083)
XLA Ops:
  7.2 0.0 all-reduce.5.cloned.1.call-start
  7.2 8.0 %convolution_select_fusion.7 = f32[256,4096]{1,0:T(8,128)} fusion(f32[1,1,256,4096]{3,2,1,0:T(8,128)} %param.3, pred[]{:T(512)S(6)} %eq.12, f32[4,256,256]{2,1,0:T(8,128)} %param.5), kind=kOutput, calls=%fused_computation.11 | convolution fusion | flops 3222274048 | bytes 8650753 | tf_op jit(solution)/shard_map/dot_general | solution.py:34
  15.2 0.0 copy-start.6
  15.2 0.0 all-reduce.5.cloned.1.call-update
  15.3 0.0 all-reduce.7.cloned.1.call-start
  15.3 0.0 copy-start.5
  15.3 154.0 %all-reduce.5.cloned.1.call-done = f32[256,4096]{1,0:T(8,128)} async-done(((f32[256,4096]{1,0:T(8,128)}), f32[256,4096]{1,0:T(8,128)}) %all-reduce.5.cloned.1.call-update) | async-done | bytes 4194320 | tf_op jit(solution)/shard_map/psum | solution.py:9
  169.3 0.0 copy-done.6
  169.3 4.2 fusion.10
  173.5 0.0 copy-start.3
  173.5 2.0 copy-done.3
  175.5 0.0 copy-done.5
  175.5 5.4 fusion.2
  180.9 0.0 all-reduce.7.cloned.1.call-update
  180.9 0.0 all-reduce.9.cloned.1.call-start
  181.0 152.5 %all-reduce.7.cloned.1.call-done = f32[256,4096]{1,0:T(8,128)} async-done(((f32[256,4096]{1,0:T(8,128)}), f32[256,4096]{1,0:T(8,128)}) %all-reduce.7.cloned.1.call-update) | async-done | bytes 4194320 | tf_op jit(solution)/shard_map/psum | solution.py:9
  333.5 4.2 fusion.9
  337.7 0.0 copy-start.2
  337.7 2.0 copy-done.2
  339.7 5.4 fusion.1
  345.1 0.0 all-reduce.9.cloned.1.call-update
  345.1 0.2 all-reduce.11.cloned.1.call-start
  345.3 152.4 %all-reduce.9.cloned.1.call-done = f32[256,4096]{1,0:T(8,128)} async-done(((f32[256,4096]{1,0:T(8,128)}), f32[256,4096]{1,0:T(8,128)}) %all-reduce.9.cloned.1.call-update) | async-done | bytes 4194320 | tf_op jit(solution)/shard_map/psum | solution.py:9
  497.7 4.2 fusion.8
  501.9 0.0 copy-start
  501.9 1.9 copy-done
  503.9 5.4 fusion
  509.2 0.0 all-reduce.11.cloned.1.call-update
  509.3 152.6 %all-reduce.11.cloned.1.call-done = f32[256,4096]{1,0:T(8,128)} async-done(((f32[256,4096]{1,0:T(8,128)}), f32[256,4096]{1,0:T(8,128)}) %all-reduce.11.cloned.1.call-update) | async-done | bytes 4194320 | tf_op jit(solution)/shard_map/psum | solution.py:9
  661.8 0.0 copy-start.1
  661.8 0.0 copy-start.4
  661.8 13.1 %pad_maximum_fusion = f32[1024,4096]{1,0:T(8,128)} fusion(f32[256,4096]{1,0:T(8,128)} %all-reduce.11.cloned.1.call-done, f32[256,4096]{1,0:T(8,128)} %all-reduce.9.cloned.1.call-done, f32[256,4096]{1,0:T(8,128)} %all-reduce.7.cloned.1.call-done, f32[256,4096]{1,0:T(8,128)} %all-reduce.5.cloned.1.call-done), kind=kLoop, calls=%fused_computation | loop fusion | flops 12582912 | bytes 33554432 | tf_op jit(solution)/shard_map/concatenate | solution.py:43
  674.9 0.0 copy-done.1
  674.9 0.0 copy-done.4
  675.0 2.7 fusion.7
Async XLA Ops:
  7.2 162.1 %all-reduce.5.cloned.1.call-start = ((), (), s32[]{:S(2)}) async-start(), calls=%async_computation | async-start | bytes 8388608 | tf_op jit(solution)/shard_map/psum | solution.py:9
  15.2 154.0 %copy-start.6 = (bf16[1,1,256,1024]{3,2,1,0:T(8,128)(2,1)S(1)}, bf16[1,1,256,1024]{3,2,1,0:T(8,128)(2,1)}, u32[]{:S(2)}) copy-start(bf16[1,1,256,1024]{3,2,1,0:T(8,128)(2,1)} %param.4) | copy-start | bytes 1572868
  15.3 318.2 %all-reduce.7.cloned.1.call-start = ((), (), s32[]{:S(2)}) async-start(), calls=%async_computation.1 | async-start | bytes 8388608 | tf_op jit(solution)/shard_map/psum | solution.py:9
  15.3 160.2 %copy-start.5 = (f32[4,256,256]{2,1,0:T(8,128)S(1)}, f32[4,256,256]{2,1,0:T(8,128)}, u32[]{:S(2)}) copy-start(f32[4,256,256]{2,1,0:T(8,128)} %param.5) | copy-start | bytes 3145732
  173.5 2.0 copy-start.3
  180.9 316.8 %all-reduce.9.cloned.1.call-start = ((), (), s32[]{:S(2)}) async-start(), calls=%async_computation.2 | async-start | bytes 8388608 | tf_op jit(solution)/shard_map/psum | solution.py:9
  337.7 2.0 copy-start.2
  345.1 316.7 %all-reduce.11.cloned.1.call-start = ((), (), s32[]{:S(2)}) async-start(), calls=%async_computation.3 | async-start | bytes 8388608 | tf_op jit(solution)/shard_map/psum | solution.py:9
  501.9 1.9 copy-start
  661.8 13.1 %copy-start.1 = (f32[1,1,256,4096]{3,2,1,0:T(8,128)S(1)}, f32[1,1,256,4096]{3,2,1,0:T(8,128)}, u32[]{:S(2)}) copy-start(f32[1,1,256,4096]{3,2,1,0:T(8,128)} %copy-done) | copy-start | bytes 12582916
  661.8 13.1 %copy-start.4 = (f32[256,4096]{1,0:T(8,128)S(1)}, f32[256,4096]{1,0:T(8,128)}, u32[]{:S(2)}) copy-start(f32[256,4096]{1,0:T(8,128)} %all-reduce.11.cloned.1.call-done) | copy-start | bytes 12582916
Sparse Core Ops, SparseCore 0:
  15.4 153.8 all-reduce.4
  181.0 152.4 all-reduce.6
  345.2 152.4 all-reduce.8
  509.4 152.4 all-reduce.10
where the time goes:
time: 688 us; the launch traced here: 684 us
  waiting for transfers between devices  612 us (89%)
  matrix products  39.4 us (6%)
  between operations  13.9 us (2%)
  other arithmetic  13.1 us (2%)
    psum x4, waiting for transfers between devices, spread(): return lax.psum(block, axis)  611 us
    dot_general x4, matrix products, body(): jnp.dot(diag_inverse[step], work[0, 0], precision=lax.Precision.HIGHEST,...  24.2 us
    dot_general x4, matrix products, apply_step(): jnp.dot(columns, solved_low, preferred_element_type=jnp.float32)  15.3 us
  transfers between devices with their start and end apart: 4, of which 4 were waited for; matrix products, arithmetic and copies ran while one was open for 0% of the time, Pallas kernels for 0%

commit v1 on v0

v1 whole, which is shorter than its diff:
```python
import jax
import jax.numpy as jnp
from jax import lax
from jax.experimental import pallas as pl
from jax.experimental.pallas import tpu as pltpu
from jax.sharding import PartitionSpec as P

MESH = pl.DeviceIdType.MESH
NB = 256
TW = 128
TILES = 32
PER = 8
CHUNKS = TILES // PER
ROOTS = 2
LAG = 4
KINDS = (("y", 1), ("z", 1), ("x", 0), ("y", 3), ("z", 3), ("x", 1), ("y", 2), ("z", 2))
PLANE = {"x": ("z", "y"), "y": ("z", "x"), "z": ("y", "x")}


def place():
    row, col = lax.axis_index("row"), lax.axis_index("col")
    return {"z": row // 4, "y": row % 4, "x": col // 2}, col % 2


def device(at, core):
    return (at["z"] * 4 + at["y"], at["x"] * 2 + core)


def moved(at, axis, by):
    new = dict(at)
    new[axis] = (at[axis] + by) % 4
    return new


def spread_kernel(
    rhs, panel, dinv, buf, rhs_v, panel_v, dinv_v, local, got, sent_b, sent_c, sent_a, sent_core
):
    at, core = place()
    me = lax.axis_index("row") * 8 + lax.axis_index("col")

    def send(block, tile, sem, to):
        pltpu.make_async_remote_copy(
            src_ref=buf.at[block, tile],
            dst_ref=buf.at[block, tile],
            send_sem=sem,
            recv_sem=got.at[block, tile],
            device_id=to,
            device_id_type=MESH,
        ).start()

    def take(block, tile):
        ref = buf.at[block, tile]
        pltpu.make_async_copy(ref, ref, got.at[block, tile]).wait()

    def drain(sem, count):
        ref = buf.at[0, pl.ds(0, count)]
        pltpu.make_async_copy(ref, ref, sem).wait()

    def rhs_copy(chunk):
        cols = pl.ds(pl.multiple_of(chunk * PER * TW, PER * TW), PER * TW)
        return pltpu.make_async_copy(rhs.at[:, cols], rhs_v.at[:, cols], local.at[chunk])

    panel_copy = pltpu.make_async_copy(panel, panel_v, local.at[CHUNKS])

    def dinv_copy(block):
        return pltpu.make_async_copy(dinv.at[block], dinv_v, local.at[CHUNKS + 1])

    peers = [(moved(at, axis, by), core) for axis in "xyz" for by in (1, 2, 3)]
    peers.append((at, 1 - core))
    barrier = pltpu.get_barrier_semaphore()
    for where, which in peers:
        pl.semaphore_signal(barrier, inc=1, device_id=device(where, which), device_id_type=MESH)

    @pl.when(me < 4)
    def _():
        dinv_copy(me).start()
        rhs_copy(0).start()
        panel_copy.start()
        for chunk in range(1, CHUNKS):
            rhs_copy(chunk).start()

    pl.semaphore_wait(barrier, len(peers))

    def kind(index, root):
        axis, j = KINDS[index]
        if axis == "x":
            j = 2 - root + j
        return axis, j

    def solve(owner, chunk):
        root = owner // 2
        rhs_copy(chunk).wait()

        @pl.when(chunk == 0)
        def _():
            dinv_copy(owner).wait()
            panel_copy.wait()

        for pair in range(PER // 2):
            tile = chunk * PER + 2 * pair
            for before in range(owner):
                if owner == 2 and before == 0 or owner == 3 and before == 1:
                    continue
                take(before, tile)
                take(before, tile + 1)
            cols = pl.ds(pl.multiple_of(tile * TW, 2 * TW), 2 * TW)
            work = rhs_v[:, cols]
            for before in range(owner):
                low = jnp.concatenate([buf[before, tile], buf[before, tile + 1]], axis=1)
                work = work - jnp.dot(
                    panel_v[:, before * NB : (before + 1) * NB], low, preferred_element_type=jnp.float32
                )
            solved = jnp.dot(
                dinv_v[...], work, precision=lax.Precision.HIGHEST, preferred_element_type=jnp.float32
            ).astype(jnp.bfloat16)
            for half in range(2):
                buf[owner, tile + half] = solved[:, half * TW : (half + 1) * TW]
                axis, j = kind(2 * pair + half, root)
                send(owner, tile + half, sent_b.at[root, tile + half], device(moved(at, axis, j), core))
                send(owner, tile + half, sent_core.at[root, tile + half], device(at, 1 - core))

    def roles(index, root):
        axis, j = kind(index, root)
        one, two = PLANE[axis]
        rel = {"x": (at["x"] - root + 4) % 4, "y": at["y"], "z": at["z"]}
        a, b, c = rel[axis], rel[one], rel[two]
        line = (a == j) & (b == 0) & (c == 0)
        root_here = (a == 0) & (b == 0) & (c == 0)
        edge = (a == j) & (b != 0) & (c == 0)
        inner = (a == j) & (c != 0)
        stage = jnp.where(line, 0, jnp.where(edge, 1, jnp.where(inner, 2, jnp.where(root_here, -1, 3))))
        return axis, one, two, a, stage

    def handle(index, root, chunk, stage):
        axis, one, two, a, mine = roles(index, root)
        block = 2 * root + core
        tile = chunk * PER + index

        @pl.when(mine == stage)
        def _():
            take(block, tile)

            @pl.when(mine == 0)
            def _():
                for by in (1, 3, 2):
                    send(block, tile, sent_b.at[root, tile], device(moved(at, one, by), core))

            @pl.when(mine <= 1)
            def _():
                for by in (1, 3, 2):
                    send(block, tile, sent_c.at[root, tile], device(moved(at, two, by), core))

            @pl.when(mine <= 2)
            def _():
                for by in (1, 3, 2):

                    @pl.when((mine != 0) | ((a + by) % 4 != 0))
                    def _():
                        send(block, tile, sent_a.at[root, tile], device(moved(at, axis, by), core))

            send(block, tile, sent_core.at[root, tile], device(at, 1 - core))

    def step(t, _):
        for owner in (0, 1):

            @pl.when((me == owner) & (t < CHUNKS))
            def _():
                solve(owner, t)

        def sub(stage, _):
            g = t - stage

            @pl.when((g >= 0) & (g < ROOTS * CHUNKS))
            def _():
                for index in range(PER):
                    handle(index, g // CHUNKS, g % CHUNKS, stage)

            return 0

        lax.fori_loop(0, 4, sub, 0)
        for owner in (2, 3):

            @pl.when((me == owner) & (t >= LAG - 1) & (t < LAG - 1 + CHUNKS))
            def _():
                solve(owner, t - (LAG - 1))

        return 0

    lax.fori_loop(0, ROOTS * CHUNKS + 3, step, 0)

    skip_first = (me == 1) | (me == 2) | (me == 3)

    def finish(tile, _):
        @pl.when(jnp.logical_not(skip_first))
        def _():
            take(1 - core, tile)

        @pl.when(me != 3)
        def _():
            take(3 - core, tile)

        return 0

    lax.fori_loop(0, TILES, finish, 0)

    def drain_all(chunk, _):
        for root in range(ROOTS):
            for index in range(PER):
                tile = chunk * PER + index
                _, _, _, _, mine = roles(index, root)
                drain(sent_core.at[root, tile], 1)

                @pl.when(mine == -1)
                def _():
                    drain(sent_b.at[root, tile], 1)

                @pl.when(mine == 0)
                def _():
                    drain(sent_b.at[root, tile], 3)
                    drain(sent_c.at[root, tile], 3)
                    drain(sent_a.at[root, tile], 2)

                @pl.when(mine == 1)
                def _():
                    drain(sent_c.at[root, tile], 3)
                    drain(sent_a.at[root, tile], 3)

                @pl.when(mine == 2)
                def _():
                    drain(sent_a.at[root, tile], 3)

        return 0

    lax.fori_loop(0, CHUNKS, drain_all, 0)


def spread(rhs, panel, dinv):
    any_space = pl.BlockSpec(memory_space=pl.ANY)
    rhs, panel, dinv = (pltpu.with_memory_space_constraint(array, pltpu.HBM) for array in (rhs, panel, dinv))
    sem = pltpu.SemaphoreType.DMA
    return pl.pallas_call(
        spread_kernel,
        out_shape=pltpu.VMEM((4, TILES, NB, TW), jnp.bfloat16),
        in_specs=[any_space] * 3,
        out_specs=pl.BlockSpec(memory_space=pltpu.VMEM),
        scratch_shapes=[
            pltpu.VMEM((NB, TILES * TW), jnp.float32),
            pltpu.VMEM((NB, 4 * NB), jnp.bfloat16),
            pltpu.VMEM((NB, NB), jnp.float32),
            sem((CHUNKS + 2,)),
            sem((4, TILES)),
            sem((ROOTS, TILES)),
            sem((ROOTS, TILES)),
            sem((ROOTS, TILES)),
            sem((ROOTS, TILES)),
        ],
        name="spread",
        compiler_params=pltpu.CompilerParams(
            collective_id=1, has_side_effects=True, vmem_limit_bytes=16 * 2**20
        ),
    )(rhs, panel, dinv)


GROUP = 4
WIDE = GROUP * TW
GROUPS = TILES // GROUP


def finish_kernel(buf, rhs, panel, sol, trail, stage, tstage, rhs_v, panel_v, load, out_s, out_t):
    me = lax.axis_index("row") * 8 + lax.axis_index("col")

    def rhs_copy(g):
        cols = pl.ds(g * WIDE, WIDE)
        return pltpu.make_async_copy(rhs.at[:, cols], rhs_v.at[:, cols], load.at[g])

    panel_copy = pltpu.make_async_copy(panel, panel_v, load.at[GROUPS])
    panel_copy.start()
    for g in range(GROUPS):
        rhs_copy(g).start()

    def sol_copy(g):
        return pltpu.make_async_copy(stage.at[g % 2], sol.at[:, pl.ds(g * WIDE, WIDE)], out_s.at[g % 2])

    def trail_copy(g):
        return pltpu.make_async_copy(tstage.at[g % 2], trail.at[:, pl.ds(g * WIDE, WIDE)], out_t.at[g % 2])

    for g in range(GROUPS):
        if g >= 2:
            sol_copy(g - 2).wait()
        for block in range(4):
            for i in range(GROUP):
                stage[g % 2, block * NB : (block + 1) * NB, i * TW : (i + 1) * TW] = buf[
                    block, g * GROUP + i
                ].astype(jnp.float32)
        sol_copy(g).start()
        if g == 0:
            panel_copy.wait()
            for block in range(4):
                cols = slice(block * NB, (block + 1) * NB)
                panel_v[:, cols] = jnp.where(me > block, panel_v[:, cols], jnp.zeros((NB, NB), jnp.bfloat16))
        rhs_copy(g).wait()
        if g >= 2:
            trail_copy(g - 2).wait()
        work = rhs_v[:, g * WIDE : (g + 1) * WIDE]
        for block in range(4):
            low = jnp.concatenate([buf[block, g * GROUP + i] for i in range(GROUP)], axis=1)
            work = work - jnp.dot(
                panel_v[:, block * NB : (block + 1) * NB], low, preferred_element_type=jnp.float32
            )
        tstage[g % 2] = work
        trail_copy(g).start()
    for g in (GROUPS - 2, GROUPS - 1):
        sol_copy(g).wait()
        trail_copy(g).wait()


def finish(buf, rhs, panel):
    any_space = pl.BlockSpec(memory_space=pl.ANY)
    buf = pltpu.with_memory_space_constraint(buf, pltpu.VMEM)
    return pl.pallas_call(
        finish_kernel,
        out_shape=(
            jax.ShapeDtypeStruct((4 * NB, TILES * TW), jnp.float32),
            jax.ShapeDtypeStruct((NB, TILES * TW), jnp.float32),
        ),
        in_specs=[pl.BlockSpec(memory_space=pltpu.VMEM), any_space, any_space],
        out_specs=(any_space, any_space),
        scratch_shapes=[
            pltpu.VMEM((2, 4 * NB, WIDE), jnp.float32),
            pltpu.VMEM((2, NB, WIDE), jnp.float32),
            pltpu.VMEM((NB, TILES * TW), jnp.float32),
            pltpu.VMEM((NB, 4 * NB), jnp.bfloat16),
            pltpu.SemaphoreType.DMA((GROUPS + 1,)),
            pltpu.SemaphoreType.DMA((2,)),
            pltpu.SemaphoreType.DMA((2,)),
        ],
        name="finish",
        compiler_params=pltpu.CompilerParams(vmem_limit_bytes=24 * 2**20),
    )(buf, rhs, panel)


def body(rhs, panel, diag_inverse):
    own = rhs.reshape(rhs.shape[2], rhs.shape[3])
    factor = panel.reshape(panel.shape[2], panel.shape[3])
    tiles = spread(own, factor, diag_inverse)
    solved, trailing = finish(tiles, own, factor)
    return solved, trailing.reshape(rhs.shape)


def solution(mesh):
    in_specs = (P(None, ("row", "col"), None, None), P(None, ("row", "col"), None, None), P())
    out_specs = (P(), P(None, ("row", "col"), None, None))
    return jax.shard_map(body, mesh=mesh, in_specs=in_specs, out_specs=out_specs, check_vma=False)
```

time: 688 us -> 81.7 us (0.12)
  waiting for transfers between devices: 612 us -> 0 us
  Pallas kernels: 0 us -> 80.8 us
  matrix products: 39.4 us -> 0 us
  other arithmetic: 13.1 us -> 0 us
  between operations: 13.9 us -> 0.83 us
    psum x4 -> x0, waiting for transfers between devices: 611 us -> none  [spread(): return lax.psum(block, axis)]
    pallas_call x0 -> x2, Pallas kernels: none -> 80.8 us  [the longest x1 72.7 us: spread(): pl.pallas_call(spread_kernel, out_shape=pltpu.VMEM((4, TILES, NB, TW), jn...]
    dot_general x8 -> x0, matrix products: 39.4 us -> none  [the longest x4 24.2 us: body(): jnp.dot(diag_inverse[step], work[0, 0], precision=lax.Precision.HIGHEST,...]
    concatenate x1 -> x0, other arithmetic: 13.1 us -> none  [body(): solution = jnp.concatenate(solved_list, axis=0)]
  transfers between devices with their start and end apart: 4 -> 0, of which waited for: 4 -> 0; matrix products, arithmetic and copies ran while one was open for 0% -> 0% of each run, Pallas kernels for 0% -> 0%
where the time goes in v1:
time: 81.7 us; the launch traced here: 81.6 us
  Pallas kernels  80.8 us (99%)
  between operations  0.83 us (1%)
    pallas_call x1, Pallas kernels, spread(): pl.pallas_call(spread_kernel, out_shape=pltpu.VMEM((4, TILES, NB, TW), jn...  72.7 us
    pallas_call x1, Pallas kernels, finish(): pl.pallas_call(finish_kernel, out_shape=(jax.ShapeDtypeStruct((4 * NB, TI...  8.1 us

profile of v1, /device:TPU:23, one launch (start us, length us, event | category | flops | bytes accessed | tf_op | source)
XLA Modules:
  0.0 81.6 jit_solution(15056820070438984492)
XLA Ops:
  0.6 0.0 copy-start.1
  0.6 0.0 copy-start
  0.6 72.7 %spread.1.buf = bf16[4,32,256,128]{3,2,1,0:T(8,128)(2,1)S(1)} custom-call(f32[256,4096]{1,0:T(8,128)} %bitcast.3, bf16[256,1024]{1,0:T(8,128)(2,1)} %bitcast.5, f32[4,256,256]{2,1,0:T(8,128)} %dinv.1), custom_call_target="tpu_custom_call" | custom-call | tf_op jit(solution)/shard_map/spread/pallas_call | solution.py:241
  73.3 0.0 copy-done.1
  73.3 0.0 copy-done
  73.3 8.1 %finish.1 = (f32[1024,4096]{1,0:T(8,128)}, f32[256,4096]{1,0:T(8,128)}) custom-call(bf16[4,32,256,128]{3,2,1,0:T(8,128)(2,1)S(1)} %spread.1.buf, f32[256,4096]{1,0:T(8,128)S(1)} %bitcast.4, bf16[256,1024]{1,0:T(8,128)(2,1)S(1)} %bitcast.6), custom_call_target="tpu_custom_call" | custom-call | tf_op jit(solution)/shard_map/finish/pallas_call | solution.py:320
Async XLA Ops:
  0.6 72.7 %copy-start.1 = (bf16[1,1,256,1024]{3,2,1,0:T(8,128)(2,1)S(1)}, bf16[1,1,256,1024]{3,2,1,0:T(8,128)(2,1)}, u32[]{:S(2)}) copy-start(bf16[1,1,256,1024]{3,2,1,0:T(8,128)(2,1)} %param.4) | copy-start | bytes 1572868
  0.6 72.7 %copy-start = (f32[1,1,256,4096]{3,2,1,0:T(8,128)S(1)}, f32[1,1,256,4096]{3,2,1,0:T(8,128)}, u32[]{:S(2)}) copy-start(f32[1,1,256,4096]{3,2,1,0:T(8,128)} %param.3) | copy-start | bytes 12582916

commit v2 on v1

v2 whole, which is shorter than its diff:
```python
import jax
import jax.numpy as jnp
from jax import lax
from jax.experimental import pallas as pl
from jax.experimental.pallas import tpu as pltpu
from jax.sharding import PartitionSpec as P

MESH = pl.DeviceIdType.MESH
NB = 256
TW = 128
TILES = 32
PER = 8
SIDE = PER // 2
CHUNKS = TILES // PER
ROOTS = 2
WIDTH = SIDE * TW
PIECES = 2
ROWS = NB // PIECES
UNITS = CHUNKS * PIECES
STRIDE = 2
LATE = 8
KINDS = (("y", 1), ("z", 1), ("x", 0), ("y", 3), ("z", 3), ("x", 1), ("y", 2), ("z", 2))
PLANE = {"x": ("z", "y"), "y": ("x", "z"), "z": ("y", "x")}


def place():
    row, col = lax.axis_index("row"), lax.axis_index("col")
    return {"z": row // 4, "y": row % 4, "x": col // 2}, col % 2


def device(at, core):
    return (at["z"] * 4 + at["y"], at["x"] * 2 + core)


def moved(at, axis, by):
    new = dict(at)
    new[axis] = (at[axis] + by) % 4
    return new


def split(value):
    first = value.astype(jnp.bfloat16)
    rest = value - first.astype(jnp.float32)
    second = rest.astype(jnp.bfloat16)
    third = (rest - second.astype(jnp.float32)).astype(jnp.bfloat16)
    return first, second, third


def dot(left, right):
    return jnp.dot(left, right, preferred_element_type=jnp.float32)


def spread_kernel(
    rhs, panel, dinv, buf, rhs_v, panel_v, dinv_v, parts, local, swap_out, swap_in, got, core_in, core_out, sent
):
    at, core = place()
    me = lax.axis_index("row") * 8 + lax.axis_index("col")
    sibling = device(at, 1 - core)
    first_root, second_root = me // 2 == 0, me // 2 == 1

    def spot(root, chunk, index):
        block = jnp.where(root == 0, core, 2 + index // SIDE)
        tile = chunk * PER + jnp.where(root == 0, index, core * SIDE + index % SIDE)
        return block, tile

    def send(block, tile, h, send_sem, recv_sem, to):
        piece = buf.at[block, tile, pl.ds(pl.multiple_of(h * ROWS, ROWS), ROWS)]
        pltpu.make_async_remote_copy(
            src_ref=piece,
            dst_ref=piece,
            send_sem=send_sem,
            recv_sem=recv_sem,
            device_id=to,
            device_id_type=MESH,
        ).start()

    def wait(ref, sem):
        pltpu.make_async_copy(ref, ref, sem).wait()

    def wait_tiles(count, sem):
        wait(buf.at[pl.ds(0, 2), pl.ds(0, count // 2)], sem)

    def take(root, chunk, index, h):
        wait(buf.at[0, 0, pl.ds(0, ROWS)], got.at[root, chunk * PER + index, h])

    def pass_over(root, chunk, index, h):
        block, tile = spot(root, chunk, index)
        send(block, tile, h, core_out.at[0], core_in.at[root, chunk], sibling)

    def columns(half, chunk):
        return pl.ds(pl.multiple_of(chunk * 2 * WIDTH + half * WIDTH, WIDTH), WIDTH)

    def rhs_copy(half, chunk, slot):
        return pltpu.make_async_copy(rhs.at[:, columns(half, chunk)], rhs_v.at[slot, chunk], local.at[slot, chunk])

    def rhs_swap(chunk):
        return pltpu.make_async_remote_copy(
            src_ref=rhs.at[:, columns(1 - core, chunk)],
            dst_ref=rhs_v.at[core, chunk],
            send_sem=swap_out.at[chunk],
            recv_sem=swap_in.at[chunk],
            device_id=sibling,
            device_id_type=MESH,
        )

    panel_copy = pltpu.make_async_copy(panel, panel_v.at[core], local.at[0, CHUNKS])
    panel_swap = pltpu.make_async_remote_copy(
        src_ref=panel,
        dst_ref=panel_v.at[core],
        send_sem=swap_out.at[CHUNKS],
        recv_sem=swap_in.at[CHUNKS],
        device_id=sibling,
        device_id_type=MESH,
    )
    dinv_copy = pltpu.make_async_copy(dinv.at[pl.ds(2 * lax.rem(me // 2, 2), 2)], dinv_v, local.at[1, CHUNKS])

    peers = [(moved(at, axis, by), core) for axis in "xyz" for by in (1, 2, 3)]
    peers.append((at, 1 - core))
    barrier = pltpu.get_barrier_semaphore()
    for where, which in peers:
        pl.semaphore_signal(barrier, inc=1, device_id=device(where, which), device_id_type=MESH)
    at_second = {"x": jnp.int32(1), "y": jnp.int32(0), "z": jnp.int32(0)}
    relay = (at["x"] == 0) & ((at["y"] == 0) != (at["z"] == 0))

    @pl.when(second_root)
    def _():
        for axis in "yz":
            for j in (1, 2, 3):
                where = {"x": jnp.int32(0), "y": jnp.int32(0), "z": jnp.int32(0)}
                where[axis] = jnp.int32(j)
                pl.semaphore_signal(barrier, inc=1, device_id=device(where, core), device_id_type=MESH)

    def split_dinv():
        dinv_copy.wait()
        for i in range(2):
            one, two, three = split(dinv_v[i])
            for n, part in enumerate((one, one, one, two, two, three)):
                parts[i, :, n * NB : (n + 1) * NB] = part

    def product(i, work):
        one, two, three = split(work)
        right = jnp.concatenate([one, two, three, one, two, one], axis=0)
        return dot(parts[i], right).astype(jnp.bfloat16)

    def keep(block, tile, solved):
        for n in range(SIDE):
            buf[block, tile + n] = solved[:, n * TW : (n + 1) * TW]

    @pl.when(first_root)
    def _():
        dinv_copy.start()
        for chunk in range(CHUNKS):
            for half in range(2):
                rhs_copy(half, chunk, half).start()
        panel_copy.start()
        split_dinv()

    @pl.when(me == 0)
    def _():
        def one(chunk, _):
            for half in range(2):
                rhs_copy(half, chunk, half).wait()
                keep(0, chunk * PER + half * SIDE, product(0, rhs_v[half, chunk]))
            return 0

        lax.fori_loop(0, CHUNKS, one, 0)
        panel_copy.wait()

    @pl.when(second_root)
    def _():
        dinv_copy.start()
        for chunk in range(CHUNKS):
            rhs_copy(core, chunk, core).start()
        panel_copy.start()
        split_dinv()

    pl.semaphore_wait(barrier, len(peers) + jnp.where(relay, 1, 0))

    @pl.when(second_root)
    def _():
        panel_swap.start()
        for chunk in range(CHUNKS):
            rhs_swap(chunk).start()

    def inject(root, chunk, index, h):
        axis, j = KINDS[index]
        if axis == "x":
            j = 2 - root + j
        block, tile = spot(root, chunk, index)
        to = device(moved(at, axis, j), core)
        send(block, tile, h, sent.at[root, 3], got.at[root, chunk * PER + index, h], to)

    @pl.when(me == 0)
    def _():
        def one(chunk, _):
            for h in range(PIECES):
                for index in range(PER):
                    pass_over(0, chunk, index, h)
                    inject(0, chunk, index, h)
            return 0

        lax.fori_loop(0, CHUNKS, one, 0)

    @pl.when(me == 1)
    def _():
        def one(chunk, _):
            wait_tiles(PER, core_in.at[0, chunk])

            @pl.when(chunk == 0)
            def _():
                panel_copy.wait()

            for half in range(2):
                rhs_copy(half, chunk, half).wait()
                first = chunk * PER + half * SIDE
                low = jnp.concatenate([buf[0, first + n] for n in range(SIDE)], axis=1)
                keep(1, first, product(1, rhs_v[half, chunk] - dot(panel_v[1, :, :NB], low)))
                for h in range(PIECES):
                    for n in range(SIDE):
                        inject(0, chunk, half * SIDE + n, h)
                        pass_over(0, chunk, half * SIDE + n, h)
            return 0

        lax.fori_loop(0, CHUNKS, one, 0)

    @pl.when(second_root)
    def _():
        def one(chunk, _):
            for h in range(PIECES):
                for index in range(PER):
                    take(0, chunk, index, h)
                    pass_over(0, chunk, index, h)
            rhs_copy(core, chunk, core).wait()
            wait(rhs_v.at[0, 0], swap_in.at[chunk])

            @pl.when(chunk == 0)
            def _():
                panel_copy.wait()
                wait(panel_v.at[0], swap_in.at[CHUNKS])

            wait_tiles(PER, core_in.at[0, chunk])
            first = chunk * PER + core * SIDE
            low = [jnp.concatenate([buf[b, first + n] for n in range(SIDE)], axis=1) for b in range(2)]
            for i in range(2):
                work = rhs_v[i, chunk]
                for before, block in enumerate(low):
                    work = work - dot(panel_v[i, :, before * NB : (before + 1) * NB], block)
                solved = product(i, work)
                low.append(solved)
                keep(2 + i, first, solved)
                for h in range(PIECES):
                    for n in range(SIDE):
                        inject(1, chunk, i * SIDE + n, h)
                for h in range(PIECES):
                    for n in range(SIDE):
                        pass_over(1, chunk, i * SIDE + n, h)
            return 0

        lax.fori_loop(0, CHUNKS, one, 0)

    def role(root, axis):
        rel = {"x": (at["x"] - root + 4) % 4, "y": at["y"], "z": at["z"]}
        one, two = (rel[name] for name in PLANE[axis])
        a = rel[axis]
        if axis == "x":
            index = jnp.where(a == 2 - root, 2, 5)
            inside = (a == 2 - root) | (a == 3 - root)
        else:
            index = jnp.where(a == 1, 0, jnp.where(a == 2, 6, 3)) + (1 if axis == "z" else 0)
            inside = a != 0
        line = (one == 0) & (two == 0)
        even = jnp.where(line, 0, jnp.where(two == 0, 1, 2))
        odd = jnp.where(line, 0, jnp.where(one == 0, 1, 2))
        none = jnp.int32(-1)
        even, odd = jnp.where(inside, even, none), jnp.where(inside, odd, none)
        near = (at["x"] == 1) & (rel["z" if axis == "y" else "y"] == 0) if root == 0 and axis != "x" else False
        return a, index, inside, line, (one != 0) & (two != 0), even, odd, near

    table = {axis: [role(root, axis) for root in range(ROOTS)] for axis in "xyz"}
    here = [(at["x"] == root) & (at["y"] == 0) & (at["z"] == 0) for root in range(ROOTS)]

    def forward(axis, root, chunk, h, stage):
        first = root == 0
        parity = chunk % 2 == 0
        pick = [jnp.where(first, p, q) for p, q in zip(table[axis][0][:2], table[axis][1][:2])]
        a, index = pick
        even, odd = (jnp.where(first, table[axis][0][n], table[axis][1][n]) for n in (5, 6))
        mine = jnp.where(parity, even, odd)
        near = first & table[axis][0][7]
        one, two = PLANE[axis]
        index_axis = "xyz".index(axis)

        @pl.when(mine == stage)
        def _():
            block, tile = spot(root, chunk, index)
            sem = sent.at[root, index_axis]
            arrived = got.at[root, chunk * PER + index, h]
            take(root, chunk, index, h)

            def along(p, q, by):
                p, q = device(moved(at, p, by), core), device(moved(at, q, by), core)
                return tuple(jnp.where(parity, i, j) for i, j in zip(p, q))

            if axis != "x":

                @pl.when((stage == 0) & first)
                def _():
                    send(block, tile, h, sem, arrived, device(at_second, core))

            @pl.when(stage == 0)
            def _():
                for by in (1, 3, 2):
                    send(block, tile, h, sem, arrived, along(one, two, by))

            @pl.when(stage <= 1)
            def _():
                for by in (1, 3, 2):
                    send(block, tile, h, sem, arrived, along(two, one, by))

            for by in (1, 3, 2):

                @pl.when(((stage != 0) & jnp.logical_not(near)) | ((a + by) % 4 != 0))
                def _():
                    send(block, tile, h, sem, arrived, device(moved(at, axis, by), core))

            pass_over(root, chunk, index, h)

    def receive(index, root, chunk, h):
        axis, j = KINDS[index]
        a = jnp.where(root == 0, table[axis][0][0], table[axis][1][0])
        if axis == "x":
            j = 2 - root + j
        at_root = jnp.where(root == 0, here[0], here[1])

        @pl.when((a != j) & jnp.logical_not(at_root))
        def _():
            take(root, chunk, index, h)
            pass_over(root, chunk, index, h)

    def unit(g):
        return g // UNITS, g % UNITS // PIECES, g % PIECES

    def step(t, _):
        def sub(stage, _):
            g = t - STRIDE * stage

            @pl.when((g >= 0) & (g < ROOTS * UNITS) & jnp.logical_not(second_root & (g < UNITS)))
            def _():
                root, chunk, h = unit(g)
                for axis in "xyz":
                    forward(axis, root, chunk, h, stage)

            return 0

        lax.fori_loop(0, 3, sub, 0)
        g = t - LATE

        @pl.when((g >= 0) & (g < ROOTS * UNITS) & jnp.logical_not(second_root & (g < UNITS)))
        def _():
            root, chunk, h = unit(g)
            for index in range(PER):
                receive(index, root, chunk, h)

        return 0

    lax.fori_loop(0, ROOTS * UNITS + LATE, step, 0)

    for chunk in range(CHUNKS):

        @pl.when((me == 0) | (me > 3))
        def _():
            wait_tiles(PER, core_in.at[0, chunk])

        wait_tiles(PER, core_in.at[1, chunk])

    wait_tiles(2 * TILES, core_out.at[0])
    for root in range(ROOTS):

        @pl.when(here[root])
        def _():
            wait_tiles(TILES, sent.at[root, 3])

        for n, axis in enumerate("xyz"):
            _, _, inside, line, inner, _, _, near = table[axis][root]
            sem = sent.at[root, n]
            straight = root == 0 and axis != "x"

            @pl.when(inside & line)
            def _():
                wait_tiles(CHUNKS * (9 if straight else 8), sem)

            @pl.when(inside & inner)
            def _():
                wait_tiles(CHUNKS * 3, sem)

            edge = inside & jnp.logical_not(line | inner)

            @pl.when(edge & jnp.logical_not(near))
            def _():
                wait_tiles(CHUNKS // 2 * 9, sem)

            if straight:

                @pl.when(edge & near)
                def _():
                    wait_tiles(CHUNKS // 2 * 7, sem)

    @pl.when(second_root)
    def _():
        panel_swap.wait_send()
        for chunk in range(CHUNKS):
            rhs_swap(chunk).wait_send()


def spread(rhs, panel, dinv):
    any_space = pl.BlockSpec(memory_space=pl.ANY)
    rhs, panel, dinv = (pltpu.with_memory_space_constraint(array, pltpu.HBM) for array in (rhs, panel, dinv))
    sem = pltpu.SemaphoreType.DMA
    return pl.pallas_call(
        spread_kernel,
        out_shape=pltpu.VMEM((4, TILES, NB, TW), jnp.bfloat16),
        in_specs=[any_space] * 3,
        out_specs=pl.BlockSpec(memory_space=pltpu.VMEM),
        scratch_shapes=[
            pltpu.VMEM((2, CHUNKS, NB, WIDTH), jnp.float32),
            pltpu.VMEM((2, NB, 4 * NB), jnp.bfloat16),
            pltpu.VMEM((2, NB, NB), jnp.float32),
            pltpu.VMEM((2, NB, 6 * NB), jnp.bfloat16),
            sem((2, CHUNKS + 1)),
            sem((CHUNKS + 1,)),
            sem((CHUNKS + 1,)),
            sem((ROOTS, TILES, PIECES)),
            sem((ROOTS, CHUNKS)),
            sem((1,)),
            sem((ROOTS, 4)),
        ],
        name="spread",
        compiler_params=pltpu.CompilerParams(
            collective_id=1, has_side_effects=True, vmem_limit_bytes=16 * 2**20
        ),
    )(rhs, panel, dinv)


GROUP = 4
WIDE = GROUP * TW
GROUPS = TILES // GROUP


def finish_kernel(buf, rhs, panel, sol, trail, stage, tstage, rhs_v, panel_v, load, out_s, out_t):
    me = lax.axis_index("row") * 8 + lax.axis_index("col")

    def rhs_copy(g):
        cols = pl.ds(g * WIDE, WIDE)
        return pltpu.make_async_copy(rhs.at[:, cols], rhs_v.at[:, cols], load.at[g])

    panel_copy = pltpu.make_async_copy(panel, panel_v, load.at[GROUPS])
    panel_copy.start()
    for g in range(GROUPS):
        rhs_copy(g).start()

    def sol_copy(g):
        return pltpu.make_async_copy(stage.at[g % 2], sol.at[:, pl.ds(g * WIDE, WIDE)], out_s.at[g % 2])

    def trail_copy(g):
        return pltpu.make_async_copy(tstage.at[g % 2], trail.at[:, pl.ds(g * WIDE, WIDE)], out_t.at[g % 2])

    for g in range(GROUPS):
        if g >= 2:
            sol_copy(g - 2).wait()
        for block in range(4):
            for i in range(GROUP):
                stage[g % 2, block * NB : (block + 1) * NB, i * TW : (i + 1) * TW] = buf[
                    block, g * GROUP + i
                ].astype(jnp.float32)
        sol_copy(g).start()
        if g == 0:
            panel_copy.wait()
            for block in range(4):
                cols = slice(block * NB, (block + 1) * NB)
                panel_v[:, cols] = jnp.where(me > block, panel_v[:, cols], jnp.zeros((NB, NB), jnp.bfloat16))
        rhs_copy(g).wait()
        if g >= 2:
            trail_copy(g - 2).wait()
        work = rhs_v[:, g * WIDE : (g + 1) * WIDE]
        for block in range(4):
            low = jnp.concatenate([buf[block, g * GROUP + i] for i in range(GROUP)], axis=1)
            work = work - jnp.dot(
                panel_v[:, block * NB : (block + 1) * NB], low, preferred_element_type=jnp.float32
            )
        tstage[g % 2] = work
        trail_copy(g).start()
    for g in (GROUPS - 2, GROUPS - 1):
        sol_copy(g).wait()
        trail_copy(g).wait()


def finish(buf, rhs, panel):
    any_space = pl.BlockSpec(memory_space=pl.ANY)
    buf = pltpu.with_memory_space_constraint(buf, pltpu.VMEM)
    return pl.pallas_call(
        finish_kernel,
        out_shape=(
            jax.ShapeDtypeStruct((4 * NB, TILES * TW), jnp.float32),
            jax.ShapeDtypeStruct((NB, TILES * TW), jnp.float32),
        ),
        in_specs=[pl.BlockSpec(memory_space=pltpu.VMEM), any_space, any_space],
        out_specs=(any_space, any_space),
        scratch_shapes=[
            pltpu.VMEM((2, 4 * NB, WIDE), jnp.float32),
            pltpu.VMEM((2, NB, WIDE), jnp.float32),
            pltpu.VMEM((NB, TILES * TW), jnp.float32),
            pltpu.VMEM((NB, 4 * NB), jnp.bfloat16),
            pltpu.SemaphoreType.DMA((GROUPS + 1,)),
            pltpu.SemaphoreType.DMA((2,)),
            pltpu.SemaphoreType.DMA((2,)),
        ],
        name="finish",
        compiler_params=pltpu.CompilerParams(vmem_limit_bytes=24 * 2**20),
    )(buf, rhs, panel)


def body(rhs, panel, diag_inverse):
    own = rhs.reshape(rhs.shape[2], rhs.shape[3])
    factor = panel.reshape(panel.shape[2], panel.shape[3])
    tiles = spread(own, factor, diag_inverse)
    solved, trailing = finish(tiles, own, factor)
    return solved, trailing.reshape(rhs.shape)


def solution(mesh):
    in_specs = (P(None, ("row", "col"), None, None), P(None, ("row", "col"), None, None), P())
    out_specs = (P(), P(None, ("row", "col"), None, None))
    return jax.shard_map(body, mesh=mesh, in_specs=in_specs, out_specs=out_specs, check_vma=False)
```

time: 81.7 us -> 62.6 us (0.77)
  Pallas kernels: 80.8 us -> 61.4 us
    pallas_call x1, Pallas kernels: 72.7 us -> 53.5 us  [spread(): pl.pallas_call(spread_kernel, out_shape=pltpu.VMEM((4, TILES, NB, TW), jn...]
where the time goes in v2:
time: 62.6 us; the launch traced here: 62.1 us
  Pallas kernels  61.4 us (98%)
  between operations  0.67 us (1%)
    pallas_call x1, Pallas kernels, spread(): pl.pallas_call(spread_kernel, out_shape=pltpu.VMEM((4, TILES, NB, TW), jn...  53.5 us
    pallas_call x1, Pallas kernels, finish(): pl.pallas_call(finish_kernel, out_shape=(jax.ShapeDtypeStruct((4 * NB, TI...  7.94 us

profile of v2, /device:TPU:23, one launch (start us, length us, event | category | flops | bytes accessed | tf_op | source)
XLA Modules:
  0.0 62.1 jit_solution(9839697540628900251)
XLA Ops:
  0.6 0.0 copy-start.1
  0.6 0.0 copy-start
  0.6 53.5 %spread.1.buf = bf16[4,32,256,128]{3,2,1,0:T(8,128)(2,1)S(1)} custom-call(f32[256,4096]{1,0:T(8,128)} %bitcast.3, bf16[256,1024]{1,0:T(8,128)(2,1)} %bitcast.5, f32[4,256,256]{2,1,0:T(8,128)} %dinv.1), custom_call_target="tpu_custom_call" | custom-call | tf_op jit(solution)/shard_map/spread/pallas_call | solution.py:419
  54.1 0.0 copy-done.1
  54.1 0.0 copy-done
  54.1 7.9 %finish.1 = (f32[1024,4096]{1,0:T(8,128)}, f32[256,4096]{1,0:T(8,128)}) custom-call(bf16[4,32,256,128]{3,2,1,0:T(8,128)(2,1)S(1)} %spread.1.buf, f32[256,4096]{1,0:T(8,128)S(1)} %bitcast.4, bf16[256,1024]{1,0:T(8,128)(2,1)S(1)} %bitcast.6), custom_call_target="tpu_custom_call" | custom-call | tf_op jit(solution)/shard_map/finish/pallas_call | solution.py:500
Async XLA Ops:
  0.6 53.5 %copy-start.1 = (bf16[1,1,256,1024]{3,2,1,0:T(8,128)(2,1)S(1)}, bf16[1,1,256,1024]{3,2,1,0:T(8,128)(2,1)}, u32[]{:S(2)}) copy-start(bf16[1,1,256,1024]{3,2,1,0:T(8,128)(2,1)} %param.4) | copy-start | bytes 1572868
  0.6 53.5 %copy-start = (f32[1,1,256,4096]{3,2,1,0:T(8,128)S(1)}, f32[1,1,256,4096]{3,2,1,0:T(8,128)}, u32[]{:S(2)}) copy-start(f32[1,1,256,4096]{3,2,1,0:T(8,128)} %param.3) | copy-start | bytes 12582916

commit v3 on v2

--- a/solution.py
+++ b/solution.py
@@ -17,8 +17,9 @@
 PIECES = 2
 ROWS = NB // PIECES
 UNITS = CHUNKS * PIECES
-STRIDE = 2
-LATE = 8
+STRIDE = 4
+LATE = 14
+WINDOW = 1
 KINDS = (("y", 1), ("z", 1), ("x", 0), ("y", 3), ("z", 3), ("x", 1), ("y", 2), ("z", 2))
 PLANE = {"x": ("z", "y"), "y": ("x", "z"), "z": ("y", "x")}
 
@@ -51,7 +52,7 @@
 
 
 def spread_kernel(
-    rhs, panel, dinv, buf, rhs_v, panel_v, dinv_v, parts, local, swap_out, swap_in, got, core_in, core_out, sent
+    rhs, panel, dinv, buf, rhs_v, panel_v, dinv_v, parts, mixed, local, swap_out, swap_in, got, core_in, core_out, sent, sent_root
 ):
     at, core = place()
     me = lax.axis_index("row") * 8 + lax.axis_index("col")
@@ -87,6 +88,17 @@
         block, tile = spot(root, chunk, index)
         send(block, tile, h, core_out.at[0], core_in.at[root, chunk], sibling)
 
+    def pass_row(root, chunk, block, first, count):
+        row = buf.at[block, pl.ds(first, count)]
+        pltpu.make_async_remote_copy(
+            src_ref=row,
+            dst_ref=row,
+            send_sem=core_out.at[0],
+            recv_sem=core_in.at[root, chunk],
+            device_id=sibling,
+            device_id_type=MESH,
+        ).start()
+
     def columns(half, chunk):
         return pl.ds(pl.multiple_of(chunk * 2 * WIDTH + half * WIDTH, WIDTH), WIDTH)
 
@@ -140,7 +152,18 @@
     def product(i, work):
         one, two, three = split(work)
         right = jnp.concatenate([one, two, three, one, two, one], axis=0)
-        return dot(parts[i], right).astype(jnp.bfloat16)
+        return dot(parts[i], right)
+
+    def mix(i, width):
+        factor = panel_v[i, :, :width]
+        exact = sum(dot(parts[i, :, n * NB : (n + 1) * NB], factor) for n in (0, 3, 5))
+        one, two, _ = split(exact)
+        mixed[i, :, :width] = one
+        mixed[i, :, width : 2 * width] = two
+
+    def solve(i, start, low):
+        width = NB * len(low)
+        return (start - dot(mixed[i, :, : 2 * width], jnp.concatenate(low + low, axis=0))).astype(jnp.bfloat16)
 
     def keep(block, tile, solved):
         for n in range(SIDE):
@@ -160,11 +183,24 @@
         def one(chunk, _):
             for half in range(2):
                 rhs_copy(half, chunk, half).wait()
-                keep(0, chunk * PER + half * SIDE, product(0, rhs_v[half, chunk]))
+                keep(0, chunk * PER + half * SIDE, product(0, rhs_v[half, chunk]).astype(jnp.bfloat16))
             return 0
 
         lax.fori_loop(0, CHUNKS, one, 0)
         panel_copy.wait()
+
+    @pl.when(me == 1)
+    def _():
+        panel_copy.wait()
+        mix(1, NB)
+
+        def one(chunk, _):
+            for half in range(2):
+                rhs_copy(half, chunk, half).wait()
+                rhs_v[half, chunk] = product(1, rhs_v[half, chunk])
+            return 0
+
+        lax.fori_loop(0, CHUNKS, one, 0)
 
     @pl.when(second_root)
     def _():
@@ -188,14 +224,18 @@
             j = 2 - root + j
         block, tile = spot(root, chunk, index)
         to = device(moved(at, axis, j), core)
-        send(block, tile, h, sent.at[root, 3], got.at[root, chunk * PER + index, h], to)
+        send(block, tile, h, sent_root.at[chunk], got.at[root, chunk * PER + index, h], to)
 
     @pl.when(me == 0)
     def _():
         def one(chunk, _):
+            @pl.when(chunk >= WINDOW)
+            def _():
+                wait_tiles(PER, sent_root.at[chunk - WINDOW])
+
+            pass_row(0, chunk, 0, chunk * PER, PER)
             for h in range(PIECES):
                 for index in range(PER):
-                    pass_over(0, chunk, index, h)
                     inject(0, chunk, index, h)
             return 0
 
@@ -205,55 +245,50 @@
     def _():
         def one(chunk, _):
             wait_tiles(PER, core_in.at[0, chunk])
-
-            @pl.when(chunk == 0)
-            def _():
-                panel_copy.wait()
-
             for half in range(2):
-                rhs_copy(half, chunk, half).wait()
                 first = chunk * PER + half * SIDE
                 low = jnp.concatenate([buf[0, first + n] for n in range(SIDE)], axis=1)
-                keep(1, first, product(1, rhs_v[half, chunk] - dot(panel_v[1, :, :NB], low)))
+                keep(1, first, solve(1, rhs_v[half, chunk], [low]))
                 for h in range(PIECES):
                     for n in range(SIDE):
                         inject(0, chunk, half * SIDE + n, h)
-                        pass_over(0, chunk, half * SIDE + n, h)
+                pass_row(0, chunk, 1, first, SIDE)
             return 0
 
         lax.fori_loop(0, CHUNKS, one, 0)
 
     @pl.when(second_root)
     def _():
+        panel_copy.wait()
+        wait(panel_v.at[0], swap_in.at[CHUNKS])
+        mix(0, 2 * NB)
+        mix(1, 3 * NB)
+
+        def start(chunk, _):
+            rhs_copy(core, chunk, core).wait()
+            wait(rhs_v.at[0, 0], swap_in.at[chunk])
+            for i in range(2):
+                rhs_v[i, chunk] = product(i, rhs_v[i, chunk])
+            return 0
+
+        lax.fori_loop(0, CHUNKS, start, 0)
+
         def one(chunk, _):
             for h in range(PIECES):
                 for index in range(PER):
                     take(0, chunk, index, h)
                     pass_over(0, chunk, index, h)
-            rhs_copy(core, chunk, core).wait()
-            wait(rhs_v.at[0, 0], swap_in.at[chunk])
-
-            @pl.when(chunk == 0)
-            def _():
-                panel_copy.wait()
-                wait(panel_v.at[0], swap_in.at[CHUNKS])
-
             wait_tiles(PER, core_in.at[0, chunk])
             first = chunk * PER + core * SIDE
             low = [jnp.concatenate([buf[b, first + n] for n in range(SIDE)], axis=1) for b in range(2)]
             for i in range(2):
-                work = rhs_v[i, chunk]
-                for before, block in enumerate(low):
-                    work = work - dot(panel_v[i, :, before * NB : (before + 1) * NB], block)
-                solved = product(i, work)
+                solved = solve(i, rhs_v[i, chunk], low)
                 low.append(solved)
                 keep(2 + i, first, solved)
                 for h in range(PIECES):
                     for n in range(SIDE):
                         inject(1, chunk, i * SIDE + n, h)
-                for h in range(PIECES):
-                    for n in range(SIDE):
-                        pass_over(1, chunk, i * SIDE + n, h)
+                pass_row(1, chunk, 2 + i, first, SIDE)
             return 0
 
         lax.fori_loop(0, CHUNKS, one, 0)
@@ -374,11 +409,16 @@
         wait_tiles(PER, core_in.at[1, chunk])
 
     wait_tiles(2 * TILES, core_out.at[0])
+
+    @pl.when(me < 4)
+    def _():
+        for chunk in range(CHUNKS):
+
+            @pl.when((me != 0) | (chunk >= CHUNKS - WINDOW))
+            def _():
+                wait_tiles(PER, sent_root.at[chunk])
+
     for root in range(ROOTS):
-
-        @pl.when(here[root])
-        def _():
-            wait_tiles(TILES, sent.at[root, 3])
 
         for n, axis in enumerate("xyz"):
             _, _, inside, line, inner, _, _, near = table[axis][root]
@@ -426,13 +466,15 @@
             pltpu.VMEM((2, NB, 4 * NB), jnp.bfloat16),
             pltpu.VMEM((2, NB, NB), jnp.float32),
             pltpu.VMEM((2, NB, 6 * NB), jnp.bfloat16),
+            pltpu.VMEM((2, NB, 6 * NB), jnp.bfloat16),
             sem((2, CHUNKS + 1)),
             sem((CHUNKS + 1,)),
             sem((CHUNKS + 1,)),
             sem((ROOTS, TILES, PIECES)),
             sem((ROOTS, CHUNKS)),
             sem((1,)),
-            sem((ROOTS, 4)),
+            sem((ROOTS, 3)),
+            sem((CHUNKS,)),
         ],
         name="spread",
         compiler_params=pltpu.CompilerParams(
@@ -441,9 +483,11 @@
     )(rhs, panel, dinv)
 
 
-GROUP = 4
-WIDE = GROUP * TW
-GROUPS = TILES // GROUP
+BAND = 64
+BANDS = 4 * NB // BAND
+SLOTS = 4
+WIDE = PER * TW
+GROUPS = CHUNKS
 
 
 def finish_kernel(buf, rhs, panel, sol, trail, stage, tstage, rhs_v, panel_v, load, out_s, out_t):
@@ -454,43 +498,49 @@
         return pltpu.make_async_copy(rhs.at[:, cols], rhs_v.at[:, cols], load.at[g])
 
     panel_copy = pltpu.make_async_copy(panel, panel_v, load.at[GROUPS])
+
+    def sol_copy(band):
+        rows = pl.ds(band * BAND, BAND)
+        return pltpu.make_async_copy(stage.at[band % SLOTS], sol.at[rows], out_s.at[band % SLOTS])
+
+    def trail_copy(g):
+        return pltpu.make_async_copy(tstage.at[g % 2], trail.at[:, pl.ds(g * WIDE, WIDE)], out_t.at[g % 2])
+
+    def widen(band):
+        if band >= SLOTS:
+            sol_copy(band - SLOTS).wait()
+        block, first = band * BAND // NB, band * BAND % NB
+        for tile in range(TILES):
+            stage[band % SLOTS, :, tile * TW : (tile + 1) * TW] = buf[block, tile, first : first + BAND].astype(
+                jnp.float32
+            )
+        sol_copy(band).start()
+
+    def update(g):
+        rhs_copy(g).wait()
+        if g >= 2:
+            trail_copy(g - 2).wait()
+        low = [jnp.concatenate([buf[b, g * PER + i] for i in range(PER)], axis=1) for b in range(4)]
+        tstage[g % 2] = rhs_v[:, g * WIDE : (g + 1) * WIDE] - dot(panel_v[...], jnp.concatenate(low, axis=0))
+        trail_copy(g).start()
+
     panel_copy.start()
     for g in range(GROUPS):
         rhs_copy(g).start()
-
-    def sol_copy(g):
-        return pltpu.make_async_copy(stage.at[g % 2], sol.at[:, pl.ds(g * WIDE, WIDE)], out_s.at[g % 2])
-
-    def trail_copy(g):
-        return pltpu.make_async_copy(tstage.at[g % 2], trail.at[:, pl.ds(g * WIDE, WIDE)], out_t.at[g % 2])
-
+    each = BANDS // GROUPS
+    for band in range(SLOTS):
+        widen(band)
+    panel_copy.wait()
+    for block in range(4):
+        cols = slice(block * NB, (block + 1) * NB)
+        panel_v[:, cols] = jnp.where(me > block, panel_v[:, cols], jnp.zeros((NB, NB), jnp.bfloat16))
     for g in range(GROUPS):
-        if g >= 2:
-            sol_copy(g - 2).wait()
-        for block in range(4):
-            for i in range(GROUP):
-                stage[g % 2, block * NB : (block + 1) * NB, i * TW : (i + 1) * TW] = buf[
-                    block, g * GROUP + i
-                ].astype(jnp.float32)
-        sol_copy(g).start()
-        if g == 0:
-            panel_copy.wait()
-            for block in range(4):
-                cols = slice(block * NB, (block + 1) * NB)
-                panel_v[:, cols] = jnp.where(me > block, panel_v[:, cols], jnp.zeros((NB, NB), jnp.bfloat16))
-        rhs_copy(g).wait()
-        if g >= 2:
-            trail_copy(g - 2).wait()
-        work = rhs_v[:, g * WIDE : (g + 1) * WIDE]
-        for block in range(4):
-            low = jnp.concatenate([buf[block, g * GROUP + i] for i in range(GROUP)], axis=1)
-            work = work - jnp.dot(
-                panel_v[:, block * NB : (block + 1) * NB], low, preferred_element_type=jnp.float32
-            )
-        tstage[g % 2] = work
-        trail_copy(g).start()
-    for g in (GROUPS - 2, GROUPS - 1):
-        sol_copy(g).wait()
+        update(g)
+        for band in range(SLOTS + g * each, min(SLOTS + (g + 1) * each, BANDS)):
+            widen(band)
+    for band in range(BANDS - SLOTS, BANDS):
+        sol_copy(band).wait()
+    for g in range(GROUPS - 2, GROUPS):
         trail_copy(g).wait()
 
 
@@ -506,12 +556,12 @@
         in_specs=[pl.BlockSpec(memory_space=pltpu.VMEM), any_space, any_space],
         out_specs=(any_space, any_space),
         scratch_shapes=[
-            pltpu.VMEM((2, 4 * NB, WIDE), jnp.float32),
+            pltpu.VMEM((SLOTS, BAND, TILES * TW), jnp.float32),
             pltpu.VMEM((2, NB, WIDE), jnp.float32),
             pltpu.VMEM((NB, TILES * TW), jnp.float32),
             pltpu.VMEM((NB, 4 * NB), jnp.bfloat16),
             pltpu.SemaphoreType.DMA((GROUPS + 1,)),
-            pltpu.SemaphoreType.DMA((2,)),
+            pltpu.SemaphoreType.DMA((SLOTS,)),
             pltpu.SemaphoreType.DMA((2,)),
         ],
         name="finish",

time: 62.6 us -> 59.9 us (0.957)
  Pallas kernels: 61.4 us -> 58.8 us
    pallas_call x1, Pallas kernels: 53.5 us -> 51 us  [spread(): pl.pallas_call(spread_kernel, out_shape=pltpu.VMEM((4, TILES, NB, TW), jn...]
where the time goes in v3:
time: 59.9 us; the launch traced here: 59.4 us
  Pallas kernels  58.8 us (98%)
  between operations  0.67 us (1%)
    pallas_call x1, Pallas kernels, spread(): pl.pallas_call(spread_kernel, out_shape=pltpu.VMEM((4, TILES, NB, TW), jn...  51 us
    pallas_call x1, Pallas kernels, finish(): pl.pallas_call(finish_kernel, out_shape=(jax.ShapeDtypeStruct((4 * NB, TI...  7.74 us

profile of v3, /device:TPU:23, one launch (start us, length us, event | category | flops | bytes accessed | tf_op | source)
XLA Modules:
  0.0 59.4 jit_solution(7012756175813212215)
XLA Ops:
  0.6 0.0 copy-start.1
  0.6 0.0 copy-start
  0.6 51.0 %spread.1.buf = bf16[4,32,256,128]{3,2,1,0:T(8,128)(2,1)S(1)} custom-call(f32[256,4096]{1,0:T(8,128)} %bitcast.3, bf16[256,1024]{1,0:T(8,128)(2,1)} %bitcast.5, f32[4,256,256]{2,1,0:T(8,128)} %dinv.1), custom_call_target="tpu_custom_call" | custom-call | tf_op jit(solution)/shard_map/spread/pallas_call | solution.py:459
  51.7 0.0 copy-done.1
  51.7 0.0 copy-done
  51.7 7.7 %finish.1 = (f32[1024,4096]{1,0:T(8,128)}, f32[256,4096]{1,0:T(8,128)}) custom-call(bf16[4,32,256,128]{3,2,1,0:T(8,128)(2,1)S(1)} %spread.1.buf, f32[256,4096]{1,0:T(8,128)S(1)} %bitcast.4, bf16[256,1024]{1,0:T(8,128)(2,1)S(1)} %bitcast.6), custom_call_target="tpu_custom_call" | custom-call | tf_op jit(solution)/shard_map/finish/pallas_call | solution.py:550
Async XLA Ops:
  0.6 51.0 %copy-start.1 = (bf16[1,1,256,1024]{3,2,1,0:T(8,128)(2,1)S(1)}, bf16[1,1,256,1024]{3,2,1,0:T(8,128)(2,1)}, u32[]{:S(2)}) copy-start(bf16[1,1,256,1024]{3,2,1,0:T(8,128)(2,1)} %param.4) | copy-start | bytes 1572868
  0.6 51.0 %copy-start = (f32[1,1,256,4096]{3,2,1,0:T(8,128)S(1)}, f32[1,1,256,4096]{3,2,1,0:T(8,128)}, u32[]{:S(2)}) copy-start(f32[1,1,256,4096]{3,2,1,0:T(8,128)} %param.3) | copy-start | bytes 12582916

commit v4 on v3

--- a/solution.py
+++ b/solution.py
@@ -19,8 +19,9 @@
 UNITS = CHUNKS * PIECES
 STRIDE = 4
 LATE = 14
+OFFSET = 6
 WINDOW = 1
-KINDS = (("y", 1), ("z", 1), ("x", 0), ("y", 3), ("z", 3), ("x", 1), ("y", 2), ("z", 2))
+KINDS = (("y", 2), ("z", 2), ("x", 0), ("y", 1), ("z", 1), ("x", 1), ("y", 3), ("z", 3))
 PLANE = {"x": ("z", "y"), "y": ("x", "z"), "z": ("y", "x")}
 
 
@@ -301,7 +302,7 @@
             index = jnp.where(a == 2 - root, 2, 5)
             inside = (a == 2 - root) | (a == 3 - root)
         else:
-            index = jnp.where(a == 1, 0, jnp.where(a == 2, 6, 3)) + (1 if axis == "z" else 0)
+            index = jnp.where(a == 2, 0, jnp.where(a == 1, 3, 6)) + (1 if axis == "z" else 0)
             inside = a != 0
         line = (one == 0) & (two == 0)
         even = jnp.where(line, 0, jnp.where(two == 0, 1, 2))
@@ -372,33 +373,34 @@
             take(root, chunk, index, h)
             pass_over(root, chunk, index, h)
 
-    def unit(g):
-        return g // UNITS, g % UNITS // PIECES, g % PIECES
-
     def step(t, _):
-        def sub(stage, _):
-            g = t - STRIDE * stage
-
-            @pl.when((g >= 0) & (g < ROOTS * UNITS) & jnp.logical_not(second_root & (g < UNITS)))
-            def _():
-                root, chunk, h = unit(g)
+        def sub(n, _):
+            root, stage = n // 3, n % 3
+            g = t - root * OFFSET - STRIDE * stage
+
+            @pl.when((g >= 0) & (g < UNITS) & jnp.logical_not(second_root & (root == 0)))
+            def _():
                 for axis in "xyz":
-                    forward(axis, root, chunk, h, stage)
-
-            return 0
-
-        lax.fori_loop(0, 3, sub, 0)
-        g = t - LATE
-
-        @pl.when((g >= 0) & (g < ROOTS * UNITS) & jnp.logical_not(second_root & (g < UNITS)))
-        def _():
-            root, chunk, h = unit(g)
-            for index in range(PER):
-                receive(index, root, chunk, h)
-
+                    forward(axis, root, g // PIECES, g % PIECES, stage)
+
+            return 0
+
+        lax.fori_loop(0, 3 * ROOTS, sub, 0)
+
+        def last(root, _):
+            g = t - root * OFFSET - LATE
+
+            @pl.when((g >= 0) & (g < UNITS) & jnp.logical_not(second_root & (root == 0)))
+            def _():
+                for index in range(PER):
+                    receive(index, root, g // PIECES, g % PIECES)
+
+            return 0
+
+        lax.fori_loop(0, ROOTS, last, 0)
         return 0
 
-    lax.fori_loop(0, ROOTS * UNITS + LATE, step, 0)
+    lax.fori_loop(0, UNITS + OFFSET + LATE, step, 0)
 
     for chunk in range(CHUNKS):
 

time: 59.9 us -> 59.1 us (0.987)
  Pallas kernels: 58.8 us -> 57.5 us
    pallas_call x1, Pallas kernels: 51 us -> 49.8 us  [spread(): pl.pallas_call(spread_kernel, out_shape=pltpu.VMEM((4, TILES, NB, TW), jn...]
where the time goes in v4:
time: 59.1 us; the launch traced here: 58.2 us
  Pallas kernels  57.5 us (97%)
  between operations  0.67 us (1%)
    pallas_call x1, Pallas kernels, spread(): pl.pallas_call(spread_kernel, out_shape=pltpu.VMEM((4, TILES, NB, TW), jn...  49.8 us
    pallas_call x1, Pallas kernels, finish(): pl.pallas_call(finish_kernel, out_shape=(jax.ShapeDtypeStruct((4 * NB, TI...  7.74 us

profile of v4, /device:TPU:23, one launch (start us, length us, event | category | flops | bytes accessed | tf_op | source)
XLA Modules:
  0.0 58.2 jit_solution(8859475799937351038)
XLA Ops:
  0.6 0.0 copy-start.1
  0.6 0.0 copy-start
  0.6 49.8 %spread.1.buf = bf16[4,32,256,128]{3,2,1,0:T(8,128)(2,1)S(1)} custom-call(f32[256,4096]{1,0:T(8,128)} %bitcast.3, bf16[256,1024]{1,0:T(8,128)(2,1)} %bitcast.5, f32[4,256,256]{2,1,0:T(8,128)} %dinv.1), custom_call_target="tpu_custom_call" | custom-call | tf_op jit(solution)/shard_map/spread/pallas_call | solution.py:461
  50.4 0.0 copy-done.1
  50.5 0.0 copy-done
  50.5 7.7 %finish.1 = (f32[1024,4096]{1,0:T(8,128)}, f32[256,4096]{1,0:T(8,128)}) custom-call(bf16[4,32,256,128]{3,2,1,0:T(8,128)(2,1)S(1)} %spread.1.buf, f32[256,4096]{1,0:T(8,128)S(1)} %bitcast.4, bf16[256,1024]{1,0:T(8,128)(2,1)S(1)} %bitcast.6), custom_call_target="tpu_custom_call" | custom-call | tf_op jit(solution)/shard_map/finish/pallas_call | solution.py:552
Async XLA Ops:
  0.6 49.8 %copy-start.1 = (bf16[1,1,256,1024]{3,2,1,0:T(8,128)(2,1)S(1)}, bf16[1,1,256,1024]{3,2,1,0:T(8,128)(2,1)}, u32[]{:S(2)}) copy-start(bf16[1,1,256,1024]{3,2,1,0:T(8,128)(2,1)} %param.4) | copy-start | bytes 1572868
  0.6 49.8 %copy-start = (f32[1,1,256,4096]{3,2,1,0:T(8,128)S(1)}, f32[1,1,256,4096]{3,2,1,0:T(8,128)}, u32[]{:S(2)}) copy-start(f32[1,1,256,4096]{3,2,1,0:T(8,128)} %param.3) | copy-start | bytes 12582916

commit v5 on v4

--- a/solution.py
+++ b/solution.py
@@ -485,9 +485,9 @@
     )(rhs, panel, dinv)
 
 
-BAND = 64
+BAND = 32
 BANDS = 4 * NB // BAND
-SLOTS = 4
+SLOTS = 12
 WIDE = PER * TW
 GROUPS = CHUNKS
 

time: 59.1 us -> 59.1 us (level)
  no operation moved by 1% of the time
where the time goes in v5:
time: 59.1 us; the launch traced here: 58.2 us
  Pallas kernels  57.6 us (97%)
  between operations  0.67 us (1%)
    pallas_call x1, Pallas kernels, spread(): pl.pallas_call(spread_kernel, out_shape=pltpu.VMEM((4, TILES, NB, TW), jn...  49.8 us
    pallas_call x1, Pallas kernels, finish(): pl.pallas_call(finish_kernel, out_shape=(jax.ShapeDtypeStruct((4 * NB, TI...  7.77 us

profile of v5, /device:TPU:23, one launch (start us, length us, event | category | flops | bytes accessed | tf_op | source)
XLA Modules:
  0.0 58.2 jit_solution(12898342477160144453)
XLA Ops:
  0.6 0.0 copy-start.1
  0.6 0.0 copy-start
  0.6 49.8 %spread.1.buf = bf16[4,32,256,128]{3,2,1,0:T(8,128)(2,1)S(1)} custom-call(f32[256,4096]{1,0:T(8,128)} %bitcast.3, bf16[256,1024]{1,0:T(8,128)(2,1)} %bitcast.5, f32[4,256,256]{2,1,0:T(8,128)} %dinv.1), custom_call_target="tpu_custom_call" | custom-call | tf_op jit(solution)/shard_map/spread/pallas_call | solution.py:461
  50.4 0.0 copy-done.1
  50.5 0.0 copy-done
  50.5 7.8 %finish.1 = (f32[1024,4096]{1,0:T(8,128)}, f32[256,4096]{1,0:T(8,128)}) custom-call(bf16[4,32,256,128]{3,2,1,0:T(8,128)(2,1)S(1)} %spread.1.buf, f32[256,4096]{1,0:T(8,128)S(1)} %bitcast.4, bf16[256,1024]{1,0:T(8,128)(2,1)S(1)} %bitcast.6), custom_call_target="tpu_custom_call" | custom-call | tf_op jit(solution)/shard_map/finish/pallas_call | solution.py:552
Async XLA Ops:
  0.6 49.8 %copy-start.1 = (bf16[1,1,256,1024]{3,2,1,0:T(8,128)(2,1)S(1)}, bf16[1,1,256,1024]{3,2,1,0:T(8,128)(2,1)}, u32[]{:S(2)}) copy-start(bf16[1,1,256,1024]{3,2,1,0:T(8,128)(2,1)} %param.4) | copy-start | bytes 1572868
  0.6 49.8 %copy-start = (f32[1,1,256,4096]{3,2,1,0:T(8,128)S(1)}, f32[1,1,256,4096]{3,2,1,0:T(8,128)}, u32[]{:S(2)}) copy-start(f32[1,1,256,4096]{3,2,1,0:T(8,128)} %param.3) | copy-start | bytes 12582916
